TPU v7x, 32 devices: a whole 2x2x4 slice. The times are simulated.
32 devices in a mesh: prompt: 4 (over y, core), seq: 2 (over x), blk: 4 (over z).
Axes of the slice: x: 2, y: 2, z: 4, core: 2. Of those that a mesh axis runs over, the one named last changes fastest.
Arguments:
- projections: bfloat16 [3, 4, 16, 4, 64, 128], P(None, None, None, 'blk', 'seq'), may hold values from -32 to 32
- residual: bfloat16 [4, 16, 4, 64, 128], P(None, None, 'blk', 'seq'), may hold values from -6 to 6
- out_proj: bfloat16 [2048, 2048], P('blk'), may hold values from -0.125 to 0.125
- modulation: float32 [3, 4, 2048], replicated, may hold values from -4 to 4
- final_weight: bfloat16 [2048, 64], replicated, may hold values from -0.125 to 0.125
- final_bias: float32 [64], replicated, may hold values from -3 to 3
- noisy_latents: float32 [4, 4, 64, 64], P(None, 'blk', 'seq'), may hold values from -6 to 6
- step_size: float32 [4], replicated, may hold values from 0.2 to 1
- conv_weight: bfloat16 [3, 3, 3, 16, 512], replicated, may hold values from -0.3125 to 0.3125
- conv_bias: float32 [512], replicated, may hold values from -3 to 3
Outputs:
- decoded: bfloat16 [16, 4, 512, 256], P(('prompt', 'blk'), None, None, 'seq'), parts along dimension 0
There are 4 independent parts, one for each index of `prompt`. A program takes and returns all parts, laid end to end along the dimension named above; an argument that names none is the same for every part. Nothing has to cross between parts.
All inputs are finite; a program needn't handle non-finite values.
Results may differ from a plain program's by a relative error of at most 0.0075.
Values may be sent and summed in bfloat16 or wider, within the bound.
A program may use at most 64 MiB of HBM per device.

v0:
```python
import math

import jax
import jax.numpy as jnp
from jax import lax
from jax.sharding import PartitionSpec as P

HEADS = 16
LATENT_CH = 16
PATCH = 2
ROWS_DEV = 1
PATCH_COLS = 32


def extended_2(cells, sides, width):
    for axis, dim in sides:
        count = lax.axis_size(axis)
        ends = count - 1
        head = lax.slice_in_dim(cells, 0, width, axis=dim)
        tail = lax.slice_in_dim(cells, cells.shape[dim] - width, cells.shape[dim], axis=dim)
        cells = jnp.concatenate(
            [
                lax.ppermute(tail, axis, [(i, (i + 1) % count) for i in range(ends)]),
                cells,
                lax.ppermute(head, axis, [((i + 1) % count, i) for i in range(ends)]),
            ],
            axis=dim,
        )
    return cells


def initial_state(queries):
    rows_shape = queries.shape[:2]
    return (
        jnp.full(rows_shape, -jnp.inf, jnp.float32),
        jnp.zeros(rows_shape, jnp.float32),
        jnp.zeros(queries.shape, jnp.float32),
    )


def attend_keys(partial_value, queries, key_part, value_part):
    key_rows = key_part.reshape(key_part.shape[0], -1, key_part.shape[-1])
    value_rows = value_part.reshape(value_part.shape[0], -1, value_part.shape[-1])
    key_count = key_rows.shape[1]
    block_len = math.gcd(key_count, 512)
    scale_factor = queries.shape[-1] ** (-0.5)

    def one_block(offset, state):
        running_max, running_sum, accumulated = state
        key_block = lax.dynamic_slice_in_dim(key_rows, offset * block_len, block_len, 1)
        value_block = lax.dynamic_slice_in_dim(value_rows, offset * block_len, block_len, 1)
        scores = (
            jnp.einsum("nqd,nkd->nqk", queries, key_block, preferred_element_type=jnp.float32)
            * scale_factor
        )
        new_max = jnp.maximum(running_max, jnp.max(scores, axis=2))
        rescale = jnp.exp(running_max - new_max)
        weights = jnp.exp(scores - new_max[:, :, None])
        new_sum = running_sum * rescale + jnp.sum(weights, axis=2)
        product = jnp.einsum(
            "nqk,nkd->nqd",
            weights.astype(jnp.bfloat16),
            value_block,
            preferred_element_type=jnp.float32,
        )
        return (new_max, new_sum, accumulated * rescale[:, :, None] + product)

    return lax.fori_loop(0, key_count // block_len, one_block, partial_value)


def finish_state(partial_value):
    return (partial_value[2] / partial_value[1][:, :, None]).astype(jnp.bfloat16)[:, None]


def convolve(time_stack, conv_weight, conv_bias):
    row_count = time_stack.shape[3] - 2
    col_count = time_stack.shape[4]
    widened = jnp.pad(time_stack, ((0, 0), (0, 0), (0, 0), (0, 0), (1, 1)))
    shifted = []
    for t_shift in range(3):
        for y_shift in range(3):
            for x_shift in range(3):
                shifted.append(
                    widened[
                        :, t_shift, :, y_shift : y_shift + row_count, x_shift : x_shift + col_count
                    ]
                )
    columns = jnp.stack(shifted, axis=1).reshape(
        time_stack.shape[0], 27 * time_stack.shape[2], row_count * col_count
    )
    kernel = conv_weight.reshape(27 * time_stack.shape[2], conv_weight.shape[-1])
    result = (
        jnp.einsum("ko,bkp->bop", kernel, columns, preferred_element_type=jnp.float32)
        + conv_bias[None, :, None]
    )
    return result.astype(jnp.bfloat16)


def body(
    projections,
    residual,
    out_proj,
    modulation,
    final_weight,
    final_bias,
    noisy_latents,
    step_size,
    conv_weight,
    conv_bias,
):
    videos_here = projections.shape[1]
    tok_here = projections.shape[4]
    head_size = projections.shape[5]
    seq_count = lax.axis_size("seq")
    pair_major = projections.reshape(
        3, seq_count, videos_here * HEADS // seq_count, 1, tok_here, head_size
    )
    kv_frames = lax.all_gather(pair_major[1:], "blk", axis=3, tiled=True)
    received = (
        lax.all_to_all(pair_major[:1], "seq", split_axis=1, concat_axis=4, tiled=True),
        lax.all_to_all(kv_frames, "seq", split_axis=1, concat_axis=4, tiled=True),
    )
    queries = received[0][0, 0, :, 0]
    partial_value = attend_keys(
        initial_state(queries), queries, received[1][0, 0], received[1][1, 0]
    )
    attended = finish_state(partial_value)
    token_major = lax.all_to_all(attended, "seq", split_axis=2, concat_axis=0, tiled=True)
    token_major = token_major.reshape(videos_here, HEADS, 1, tok_here, head_size)
    width_all = HEADS * head_size
    token_rows = jnp.transpose(token_major, (0, 2, 3, 1, 4)).reshape(
        videos_here * tok_here, width_all
    )
    projected = jnp.dot(
        token_rows,
        lax.all_gather(out_proj, "blk", axis=0, tiled=True),
        preferred_element_type=jnp.float32,
    )
    projected = jnp.transpose(
        projected.reshape(videos_here, 1, tok_here, HEADS, head_size), (0, 3, 1, 2, 4)
    )
    factors = modulation.reshape(3, videos_here, HEADS, 1, 1, head_size)
    mixed = residual.astype(jnp.float32) + factors[2] * projected
    center = jnp.mean(mixed, axis=(1, 4), keepdims=True)
    spread = jnp.mean(jnp.square(mixed - center), axis=(1, 4), keepdims=True)
    normed = (mixed - center) * lax.rsqrt(spread + 1e-06)
    modulated = (normed * (1.0 + factors[1]) + factors[0]).astype(jnp.bfloat16)
    out_weight = final_weight.reshape(HEADS, head_size, final_weight.shape[1])
    prediction = (
        jnp.einsum("vhftd,hdo->vfto", modulated, out_weight, preferred_element_type=jnp.float32)
        + final_bias
    )
    latents = ((noisy_latents + step_size[:, None, None, None] * prediction) / 0.476986).astype(
        jnp.bfloat16
    )
    latent_image = latents.reshape(videos_here, 1, ROWS_DEV, PATCH_COLS, LATENT_CH, PATCH, PATCH)
    latent_image = jnp.transpose(latent_image, (0, 1, 4, 2, 5, 3, 6))
    latent_image = latent_image.reshape(
        videos_here, 1, LATENT_CH, PATCH * ROWS_DEV, PATCH * PATCH_COLS
    )
    tile_frames = lax.all_to_all(latent_image, "blk", split_axis=0, concat_axis=1, tiled=True)[0]
    extended = extended_2(tile_frames, (("seq", 2),), 1)
    padded = jnp.concatenate([extended[:1], extended[:1], extended], axis=0)
    frame_total = tile_frames.shape[0]
    time_stack = jnp.stack(
        [padded[0:frame_total], padded[1 : frame_total + 1], padded[2 : frame_total + 2]], axis=1
    )
    decoded = convolve(time_stack, conv_weight, conv_bias)[None]
    return decoded


def solution(mesh):
    return jax.shard_map(
        body,
        mesh=mesh,
        in_specs=(
            P(None, None, None, "blk", "seq", None),
            P(None, None, "blk", "seq", None),
            P("blk", None),
            P(),
            P(),
            P(),
            P(None, "blk", "seq", None),
            P(),
            P(),
            P(),
        ),
        out_specs=P(("prompt", "blk"), None, None, "seq"),
        check_vma=False,
    )
```

profile of v0, /device:TPU:0, one launch (start us, length us, event | category | flops | bytes accessed | tf_op | source)
XLA Modules:
  0.0 287.9 jit_solution(9785880962053328743)
XLA Ops:
  6.5 0.0 copy-start
  6.5 0.0 all-gather.3.cloned.1.call-start
  6.5 2.4 slice.189
  8.9 0.0 all-gather.3.cloned.1.call-update
  8.9 0.0 all-gather.5.cloned.1.call-start
  9.0 0.7 all-gather.5.cloned.1.call-update
  9.7 1.9 slice.149
  11.6 4.2 %all-to-all-start = ((bf16[1,2,32,1,32,128]{5,4,2,3,0,1:T(8,128)(2,1)}), bf16[1,2,32,1,32,128]{5,4,2,3,0,1:T(8,128)(2,1)S(1)}, u32[]{:S(2)}, u32[]{:S(2)}) async-start(bf16[1,2,32,1,32,128]{5,4,2,3,0,1:T(8,128)(2,1)} %bitcast.2), calls=%async_computation | async-start | bytes 1048576 | tf_op jit(solution)/shard_map/all_to_all | solution.py:120
  15.8 76.8 %all-gather.3.cloned.1.call-done = bf16[2,2,32,4,32,128]{5,4,2,1,0,3:T(8,128)(2,1)} async-done(((bf16[2,2,32,1,32,128]{5,4,2,1,0,3:T(8,128)(2,1)}), bf16[2,2,32,4,32,128]{5,4,2,1,0,3:T(8,128)(2,1)}) %all-gather.3.cloned.1.call-update) | async-done | bytes 4194320 | tf_op jit(solution)/shard_map/all_gather | solution.py:118
  92.6 5.4 %copy.149 = bf16[2,2,32,4,32,128]{5,4,3,2,0,1:T(8,128)(2,1)} copy(bf16[2,2,32,4,32,128]{5,4,2,1,0,3:T(8,128)(2,1)} %all-gather.3.cloned.1.call-done) | data formatting | bytes 8388608 | tf_op jit(solution)/shard_map/all_gather | solution.py:118
  98.0 0.0 all-to-all-done
  98.0 6.0 %all-to-all-start.1 = ((bf16[2,2,32,4,32,128]{5,4,3,2,0,1:T(8,128)(2,1)}), bf16[2,2,32,4,32,128]{5,4,3,2,0,1:T(8,128)(2,1)}, u32[]{:S(2)}, u32[]{:S(2)}) async-start(bf16[2,2,32,4,32,128]{5,4,3,2,0,1:T(8,128)(2,1)} %copy.149), calls=%async_computation.1 | async-start | bytes 8388608 | tf_op jit(solution)/shard_map/all_to_all | solution.py:121
  103.9 0.1 copy.147
  104.0 47.6 %all-to-all-done.1 = bf16[2,2,32,4,32,128]{5,4,3,2,0,1:T(8,128)(2,1)} async-done(((bf16[2,2,32,4,32,128]{5,4,3,2,0,1:T(8,128)(2,1)}), bf16[2,2,32,4,32,128]{5,4,3,2,0,1:T(8,128)(2,1)}, u32[]{:S(2)}, u32[]{:S(2)}) %all-to-all-start.1) | async-done | bytes 4194336 | tf_op jit(solution)/shard_map/all_to_all | solution.py:121
  151.6 3.1 %fusion.39 = (bf16[1,1,32,4,2,32,128]{6,5,3,2,0,4,1:T(8,128)(2,1)S(1)}, bf16[1,1,32,4,2,32,128]{6,5,3,2,0,4,1:T(8,128)(2,1)S(1)}) fusion(bf16[2,1,32,4,2,32,128]{6,5,3,2,0,4,1:T(8,128)(2,1)} %bitcast.9), kind=kLoop, calls=%fused_computation.91 | loop fusion | bytes 8388608 | tf_op jit(solution)/shard_map/slice | solution.py:125
  154.7 0.5 copy.151
  155.2 0.5 copy.150
  155.7 0.9 multiply_reduce_fusion
  156.7 0.8 fusion
  157.5 1.2 fusion.9
  158.7 0.0 copy-start.1
  158.7 1.1 copy.152
  159.8 3.5 %all-to-all-start.2 = ((bf16[32,1,64,128]{3,0,1,2:T(8,128)(2,1)}), bf16[32,1,64,128]{3,0,1,2:T(8,128)(2,1)S(1)}, u32[]{:S(2)}, u32[]{:S(2)}) async-start(bf16[32,1,64,128]{3,0,1,2:T(8,128)(2,1)} %copy.152), calls=%async_computation.2 | async-start | bytes 1048576 | tf_op jit(solution)/shard_map/all_to_all | solution.py:128
  163.3 0.0 copy-done.1
  163.4 7.3 %all-to-all-done.2 = bf16[32,1,64,128]{3,0,1,2:T(8,128)(2,1)S(1)} async-done(((bf16[32,1,64,128]{3,0,1,2:T(8,128)(2,1)}), bf16[32,1,64,128]{3,0,1,2:T(8,128)(2,1)S(1)}, u32[]{:S(2)}, u32[]{:S(2)}) %all-to-all-start.2) | async-done | bytes 524320 | tf_op jit(solution)/shard_map/all_to_all | solution.py:128
  170.7 0.2 copy.153
  170.9 0.2 copy.155
  171.1 0.2 reshape.119
  171.4 71.0 %all-gather.5.cloned.1.call-done = bf16[2048,2048]{1,0:T(8,128)(2,1)} async-done(((bf16[512,2048]{1,0:T(8,128)(2,1)}), bf16[2048,2048]{1,0:T(8,128)(2,1)}) %all-gather.5.cloned.1.call-update) | async-done | bytes 8388624 | tf_op jit(solution)/shard_map/all_gather | solution.py:136
  242.3 11.8 %copy.156 = bf16[2048,2048]{1,0:T(8,128)(2,1)} copy(bf16[2048,2048]{0,1:T(8,128)(2,1)} %bitcast.130) | data formatting | bytes 16777216 | tf_op jit(solution)/shard_map/dot_general | solution.py:134
  254.1 0.0 copy-done.3
  254.1 0.0 copy-start.6
  254.2 0.0 copy-start.7
  254.2 6.4 %fusion.41 = (f32[4,32]{1,0:T(4,128)S(1)}, f32[4,16,1,32,128]{4,3,1,0,2:T(8,128)S(1)}) fusion(bf16[16,128,2048,1]{2,1,0,3:T(8,128)(2,1)} %bitcast.131, bf16[4,32,2048,1]{2,1,0,3:T(8,128)(2,1)S(1)} %reshape.119, f32[4,16,128]{2,1,0:T(8,128)S(1)} %bitcast.143, bf16[4,16,1,32,128]{4,3,2,1,0:T(8,128)(2,1)S(1)} %copy-done.3), kind=kOutput, calls=%fused_computation.93 | convolution fusion | flops 1074790272 | bytes 10519040 | tf_op jit(solution)/shard_map/dot_general | solution.py:134
  260.6 0.3 multiply_reduce_fusion.1
  260.9 0.0 copy-done.4
  260.9 0.0 copy-done.5
  260.9 0.0 copy-done.6
  260.9 0.4 fusion.15
  261.3 0.1 copy.159
  261.4 0.1 copy.160
  261.5 0.1 copy.161
  261.6 0.1 reshape.125
  261.7 8.0 %all_to_all.54 = bf16[4,2,1024]{2,1,0:T(2,128)(2,1)S(1)} all-to-all(bf16[4,2,1024]{2,1,0:T(2,128)(2,1)S(1)} %reshape.125), channel_id=1, replica_groups=mesh['prompt'=4,'seq'=2,'blk'=4] {'blk'}, dimensions={0} | all-to-all | bytes 32768 | tf_op jit(solution)/shard_map/all_to_all | solution.py:161
  269.7 0.1 reshape.126
  269.8 1.3 collective-permute-start.1
  271.1 4.5 %collective-permute-start = (bf16[4,16,1,64]{3,1,2,0:T(8,128)(2,1)S(1)}, bf16[4,16,1,64]{3,1,2,0:T(8,128)(2,1)S(1)}, u32[]{:S(2)}, u32[]{:S(2)}) collective-permute-start(bf16[4,16,1,64]{3,1,2,0:T(8,128)(2,1)S(1)} %get-tuple-element.37), channel_id=1, source_target_pairs={{0,4},{1,5},{2,6},{3,7},{8,12},{9,13},{10,14},{11,15},{16,20},{17,... | collective-permute-start | bytes 24584 | tf_op jit(solution)/shard_map/ppermute | solution.py:23
  275.7 0.0 collective-permute-done.1
  275.7 1.4 collective-permute-done
  277.2 0.1 fusion.32
  277.3 0.1 constant_dynamic-update-slice_fusion.24
  277.5 0.1 constant_dynamic-update-slice_fusion.21
  277.6 0.1 constant_dynamic-update-slice_fusion.18
  277.7 0.0 copy-start.2
  277.7 0.1 constant_dynamic-update-slice_fusion.15
  277.8 0.1 constant_dynamic-update-slice_fusion.12
  278.0 0.1 constant_dynamic-update-slice_fusion.9
  278.1 0.1 constant_dynamic-update-slice_fusion.6
  278.2 0.1 constant_dynamic-update-slice_fusion.3
  278.3 0.1 constant_dynamic-update-slice_fusion
  278.4 0.7 copy.162
  279.1 0.4 reshape.117
  279.5 0.5 fusion.8
  280.0 1.0 copy.163
  (36 shorter events, 0.3 us)
Async XLA Ops:
  6.5 273.0 %copy-start = (bf16[3,3,3,16,512]{4,3,2,1,0:T(8,128)(2,1)S(1)}, bf16[3,3,3,16,512]{4,3,2,1,0:T(8,128)(2,1)}, u32[]{:S(2)}) copy-start(bf16[3,3,3,16,512]{4,3,2,1,0:T(8,128)(2,1)} %param.18) | copy-start | bytes 1327108
  6.5 86.0 %all-gather.3.cloned.1.call-start = ((), (), s32[]{:S(2)}) async-start(), calls=%async_computation.4 | async-start | bytes 5242880 | tf_op jit(solution)/shard_map/all_gather | solution.py:118
  8.9 233.4 %all-gather.5.cloned.1.call-start = ((), (), s32[]{:S(2)}) async-start(), calls=%async_computation.5 | async-start | bytes 10485760 | tf_op jit(solution)/shard_map/all_gather | solution.py:136
  11.6 86.4 %all-to-all-start = ((bf16[1,2,32,1,32,128]{5,4,2,3,0,1:T(8,128)(2,1)}), bf16[1,2,32,1,32,128]{5,4,2,3,0,1:T(8,128)(2,1)S(1)}, u32[]{:S(2)}, u32[]{:S(2)}) async-start(bf16[1,2,32,1,32,128]{5,4,2,3,0,1:T(8,128)(2,1)} %bitcast.2), calls=%async_computation | async-start | bytes 1048576 | tf_op jit(solution)/shard_map/all_to_all | solution.py:120
  98.0 53.6 %all-to-all-start.1 = ((bf16[2,2,32,4,32,128]{5,4,3,2,0,1:T(8,128)(2,1)}), bf16[2,2,32,4,32,128]{5,4,3,2,0,1:T(8,128)(2,1)}, u32[]{:S(2)}, u32[]{:S(2)}) async-start(bf16[2,2,32,4,32,128]{5,4,3,2,0,1:T(8,128)(2,1)} %copy.149), calls=%async_computation.1 | async-start | bytes 8388608 | tf_op jit(solution)/shard_map/all_to_all | solution.py:121
  158.7 4.6 %copy-start.1 = (f32[3,4,2048]{2,1,0:T(4,128)S(1)}, f32[3,4,2048]{2,1,0:T(4,128)}, u32[]{:S(2)}) copy-start(f32[3,4,2048]{2,1,0:T(4,128)} %param.13) | copy-start | bytes 294916
  159.8 10.8 %all-to-all-start.2 = ((bf16[32,1,64,128]{3,0,1,2:T(8,128)(2,1)}), bf16[32,1,64,128]{3,0,1,2:T(8,128)(2,1)S(1)}, u32[]{:S(2)}, u32[]{:S(2)}) async-start(bf16[32,1,64,128]{3,0,1,2:T(8,128)(2,1)} %copy.152), calls=%async_computation.2 | async-start | bytes 1048576 | tf_op jit(solution)/shard_map/all_to_all | solution.py:128
  242.3 11.8 %copy-start.3 = (bf16[4,16,1,32,128]{4,3,2,1,0:T(8,128)(2,1)S(1)}, bf16[4,16,1,32,128]{4,3,2,1,0:T(8,128)(2,1)}, u32[]{:S(2)}) copy-start(bf16[4,16,1,32,128]{4,3,2,1,0:T(8,128)(2,1)} %param.11) | copy-start | bytes 1572868
  254.1 6.7 %copy-start.4 = (bf16[2048,64]{0,1:T(8,128)(2,1)S(1)}, bf16[2048,64]{0,1:T(8,128)(2,1)}, u32[]{:S(2)}) copy-start(bf16[2048,64]{0,1:T(8,128)(2,1)} %param.14) | copy-start | bytes 786436
  254.1 6.7 %copy-start.5 = (f32[4,1,32,64]{3,2,1,0:T(8,128)S(1)}, f32[4,1,32,64]{3,2,1,0:T(8,128)}, u32[]{:S(2)}) copy-start(f32[4,1,32,64]{3,2,1,0:T(8,128)} %param.16) | copy-start | bytes 98308
  254.1 6.7 %copy-start.6 = (f32[64]{0:T(128)S(1)}, f32[64]{0:T(128)}, u32[]{:S(2)}) copy-start(f32[64]{0:T(128)} %param.15) | copy-start | bytes 772
  254.2 6.7 %copy-start.7 = (f32[4]{0:T(128)S(1)}, f32[4]{0:T(128)}, u32[]{:S(2)}) copy-start(f32[4]{0:T(128)} %param.17) | copy-start | bytes 52
  269.8 5.9 %collective-permute-start.1 = (bf16[4,16,1,64]{3,1,2,0:T(8,128)(2,1)S(1)}, bf16[4,16,1,64]{3,1,2,0:T(8,128)(2,1)S(1)}, u32[]{:S(2)}, u32[]{:S(2)}) collective-permute-start(bf16[4,16,1,64]{3,1,2,0:T(8,128)(2,1)S(1)} %get-tuple-element.38), channel_id=1, source_target_pairs={{4,0},{5,1},{6,2},{7,3},{12,8},{13,9},{14,10},{15,11},{20,16},{21,... | collective-permute-start | bytes 24584 | tf_op jit(solution)/shard_map/ppermute | solution.py:25
  271.1 6.0 %collective-permute-start = (bf16[4,16,1,64]{3,1,2,0:T(8,128)(2,1)S(1)}, bf16[4,16,1,64]{3,1,2,0:T(8,128)(2,1)S(1)}, u32[]{:S(2)}, u32[]{:S(2)}) collective-permute-start(bf16[4,16,1,64]{3,1,2,0:T(8,128)(2,1)S(1)} %get-tuple-element.37), channel_id=1, source_target_pairs={{0,4},{1,5},{2,6},{3,7},{8,12},{9,13},{10,14},{11,15},{16,20},{17,... | collective-permute-start | bytes 24584 | tf_op jit(solution)/shard_map/ppermute | solution.py:23
  277.7 1.8 copy-start.2
Sparse Core Ops, SparseCore 0:
  9.1 83.4 all-gather.2
  94.1 148.1 all-gather.4
where the time goes:
time: 289 us; the launch traced here: 288 us
  waiting for transfers between devices  205 us (71%)
  local copies, waits for them, and re-layouts  31.1 us (11%)
  starting transfers between devices  19.5 us (7%)
  between operations  13.8 us (5%)
  matrix products  9.38 us (3%)
  blocking collectives  7.96 us (3%)
    all_gather x1, waiting for transfers between devices, body(): kv_frames = lax.all_gather(pair_major[1:], 'blk', axis=3, tiled=True)  76.8 us
    all_gather x1, waiting for transfers between devices, body(): lax.all_gather(out_proj, 'blk', axis=0, tiled=True)  71 us
    all_to_all x1, waiting for transfers between devices, body(): lax.all_to_all(kv_frames, 'seq', split_axis=1, concat_axis=4, tiled=True)  47.6 us
    dot_general x1, local copies, waits for them, and re-layouts, body(): jnp.dot(token_rows, lax.all_gather(out_proj, 'blk', axis=0, tiled=True),...  11.8 us
    all_to_all x1, blocking collectives, body(): lax.all_to_all(latent_image, 'blk', split_axis=0, concat_axis=1, tiled=True)  7.96 us
    all_to_all x1, waiting for transfers between devices, body(): lax.all_to_all(attended, 'seq', split_axis=2, concat_axis=0, tiled=True)  7.28 us
    dot_general x1, matrix products, body(): jnp.dot(token_rows, lax.all_gather(out_proj, 'blk', axis=0, tiled=True),...  6.41 us
    all_to_all x1, starting transfers between devices, body(): lax.all_to_all(kv_frames, 'seq', split_axis=1, concat_axis=4, tiled=True)  5.95 us
  transfers between devices with their start and end apart: 7, of which 5 were waited for; matrix products, arithmetic and copies ran while one was open for 6% of the time, Pallas kernels for 0%

commit v1 on v0

--- a/solution.py
+++ b/solution.py
@@ -1,8 +1,11 @@
+import functools
 import math
 
 import jax
 import jax.numpy as jnp
 from jax import lax
+from jax.experimental import pallas as pl
+from jax.experimental.pallas import tpu as pltpu
 from jax.sharding import PartitionSpec as P
 
 HEADS = 16
@@ -169,9 +172,334 @@
     return decoded
 
 
+def fits(mesh):
+    return mesh.shape["seq"] == 2 and mesh.shape["blk"] == 4 and mesh.shape["prompt"] == 4
+
+
+def dot(lhs, rhs, lhs_dim=1, rhs_dim=0):
+    return lax.dot_general(
+        lhs, rhs, (((lhs_dim,), (rhs_dim,)), ((), ())), preferred_element_type=jnp.float32
+    )
+
+
+def fused_kernel(
+    proj,
+    res_in,
+    out_w,
+    noisy_in,
+    mod,
+    final_w,
+    final_b,
+    step,
+    conv_w,
+    conv_b,
+    out,
+    qkv,
+    res,
+    noisy,
+    rows,
+    att,
+    part_out,
+    part_in,
+    mixed,
+    normal,
+    image,
+    halo,
+    strip,
+    spread,
+    columns,
+    bias,
+    factors,
+    qkv_send,
+    qkv_recv,
+    res_send,
+    res_recv,
+    noisy_send,
+    noisy_recv,
+    row_send,
+    row_recv,
+    share_send,
+    share_recv,
+    part_send,
+    part_recv,
+    halo_sem,
+    local_sem,
+):
+    p, s, b = lax.axis_index("prompt"), lax.axis_index("seq"), lax.axis_index("blk")
+    other = 1 - s
+    blks = [lax.rem(b + d, 4) for d in range(4)]
+    froms = [lax.rem(b + 4 - d, 4) for d in range(4)]
+    seqs = [s, other]
+    prompts = [lax.rem(p + d, 4) for d in range(4)]
+    prompt_froms = [lax.rem(p + 4 - d, 4) for d in range(4)]
+    pairs = [(db, ds) for db in (2, 1, 3, 0) for ds in (0, 1) if (db, ds) != (0, 0)]
+
+    barrier = pltpu.get_barrier_semaphore()
+    for db, ds in pairs:
+        pl.semaphore_signal(barrier, inc=1, device_id=(p, seqs[ds], blks[db]), device_id_type=pl.DeviceIdType.MESH)
+    for dp in (1, 2, 3):
+        pl.semaphore_signal(barrier, inc=1, device_id=(prompts[dp], s, b), device_id_type=pl.DeviceIdType.MESH)
+    pl.semaphore_wait(barrier, 10)
+
+    def remote(src, dst, send, recv, target):
+        return pltpu.make_async_remote_copy(
+            src_ref=src,
+            dst_ref=dst,
+            send_sem=send,
+            recv_sem=recv,
+            device_id=target,
+            device_id_type=pl.DeviceIdType.MESH,
+        )
+
+    def row_slot(group, quarter):
+        return rows.at[pl.ds(pl.multiple_of(group * 256 + quarter * 64, 64), 64)]
+
+    def row_copy(db, source):
+        return remote(out_w.at[s, p], row_slot(source, p), row_send.at[db], row_recv.at[source], (p, s, blks[db]))
+
+    def share_copy(group, dp, source):
+        return remote(
+            row_slot(group, source),
+            row_slot(group, source),
+            share_send.at[group, dp],
+            share_recv.at[group, source],
+            (prompts[dp], s, b),
+        )
+
+    def qkv_copy(g, db, ds, frame, row):
+        return remote(
+            proj.at[:, blks[db], g, seqs[ds]],
+            qkv.at[:, g, :, frame, row],
+            qkv_send.at[g, db, ds],
+            qkv_recv.at[g, frame, row],
+            (p, seqs[ds], blks[db]),
+        )
+
+    def res_copy(db, frame):
+        return remote(res_in.at[blks[db]], res.at[:, frame], res_send.at[db], res_recv.at[frame], (p, s, blks[db]))
+
+    def noisy_copy(db, frame):
+        return remote(noisy_in.at[blks[db]], noisy.at[frame], noisy_send.at[db], noisy_recv.at[frame], (p, s, blks[db]))
+
+    for db in (2, 1, 3):
+        row_copy(db, b).start()
+    for g in range(4):
+        for db, ds in pairs:
+            qkv_copy(g, db, ds, b, s).start()
+    for db in (2, 1, 3):
+        noisy_copy(db, b).start()
+        res_copy(db, b).start()
+    own = [
+        pltpu.make_async_copy(proj.at[:, b, g, s], qkv.at[:, g, :, b, s], local_sem.at[g]) for g in range(4)
+    ]
+    own.append(pltpu.make_async_copy(res_in.at[b], res.at[:, b], local_sem.at[4]))
+    own.append(pltpu.make_async_copy(noisy_in.at[b], noisy.at[b], local_sem.at[5]))
+    for quarter in range(4):
+        own.append(pltpu.make_async_copy(out_w.at[s, quarter], row_slot(b, quarter), local_sem.at[6 + quarter]))
+    for copy in own:
+        copy.start()
+
+    for half in range(2):
+        at_row = lax.broadcasted_iota(jnp.int32, (128, 768), 0)
+        at_col = lax.broadcasted_iota(jnp.int32, (128, 768), 1)
+        same = (at_row >> 5) == ((at_col >> 6) & 3)
+        place = (at_col & 63) == 2 * (at_row & 31) + (half + 1) - (at_col >> 8)
+        spread[half * 128 : half * 128 + 128, :] = jnp.where(same & place, 1.0, 0.0).astype(jnp.bfloat16)
+    for k in range(3):
+        video = lax.broadcasted_iota(jnp.int32, (4, 2048), 0)
+        factors[k : k + 1, :] = jnp.sum(jnp.where(video == b, mod[k], 0.0), axis=0, keepdims=True)
+    bias[...] = jnp.broadcast_to(conv_b[...], (128, 512)).T
+
+    for db in (1, 3, 2):
+        row_copy(db, froms[db]).wait_recv()
+        for dp in (1, 2, 3):
+            share_copy(froms[db], dp, p).start()
+
+    scale = 128 ** (-0.5)
+    for g in range(4):
+        own[g].wait()
+        for db, ds in pairs:
+            qkv_copy(g, db, ds, froms[db], seqs[ds]).wait_recv()
+        for k in range(2):
+            q = qkv[0, g, k].reshape(256, 128)
+            key = qkv[1, g, k].reshape(256, 128)
+            value = qkv[2, g, k].reshape(256, 128)
+            scores = dot(q, key, 1, 1) * scale
+            weights = jnp.exp(scores - jnp.max(scores, axis=1, keepdims=True))
+            totals = jnp.sum(weights, axis=1, keepdims=True)
+            result = (dot(weights.astype(jnp.bfloat16), value) / totals).astype(jnp.bfloat16)
+            at = (g * 2 + k) * 128
+            for f in range(4):
+                for i in range(2):
+                    att[i, f * 32 : f * 32 + 32, at : at + 128] = result[f * 64 + i * 32 : f * 64 + i * 32 + 32]
+
+    for quarter in range(4):
+        own[6 + quarter].wait()
+    for db in (1, 3, 2):
+        for dp in (1, 2, 3):
+            share_copy(froms[db], dp, prompt_froms[dp]).wait_recv()
+
+    def part_copy(c):
+        cols = pl.ds(c * 512, 512)
+        return remote(part_out.at[:, cols], part_in.at[:, cols], part_send.at[c], part_recv.at[c], (p, other, b))
+
+    for c in range(4):
+        part_out[:, c * 512 : c * 512 + 512] = dot(att[other], rows[:, c * 512 : c * 512 + 512]).astype(jnp.bfloat16)
+        part_copy(c).start()
+    own[4].wait()
+    for db in (1, 3, 2):
+        res_copy(db, froms[db]).wait_recv()
+
+    total = jnp.zeros((128, 128), jnp.float32)
+    for c in range(4):
+        mine = dot(att[s], rows[:, c * 512 : c * 512 + 512])
+        part_copy(c).wait_recv()
+        for k in range(4):
+            h = c * 4 + k
+            at = h * 128
+            projected = mine[:, k * 128 : k * 128 + 128] + part_in[:, at : at + 128].astype(jnp.float32)
+            value = res[h].reshape(128, 128).astype(jnp.float32) + factors[2:3, at : at + 128] * projected
+            mixed[:, at : at + 128] = value
+            total = total + value
+    center = jnp.sum(total, axis=1, keepdims=True) * (1.0 / 2048)
+    total = jnp.zeros((128, 128), jnp.float32)
+    for h in range(16):
+        total = total + jnp.square(mixed[:, h * 128 : h * 128 + 128] - center)
+    inverse = lax.rsqrt(jnp.sum(total, axis=1, keepdims=True) * (1.0 / 2048) + 1e-06)
+    for h in range(16):
+        at = h * 128
+        normed = (mixed[:, at : at + 128] - center) * inverse
+        normal[:, at : at + 128] = (
+            normed * (1.0 + factors[1:2, at : at + 128]) + factors[0:1, at : at + 128]
+        ).astype(jnp.bfloat16)
+    prediction = dot(normal[...], final_w[...]) + final_b[...]
+    own[5].wait()
+    for db in (1, 3, 2):
+        noisy_copy(db, froms[db]).wait_recv()
+    latents = ((noisy[...].reshape(128, 64) + step[b] * prediction) / 0.476986).astype(jnp.bfloat16)
+
+    to = lax.broadcasted_iota(jnp.int32, (64, 64), 0)
+    channel = lax.broadcasted_iota(jnp.int32, (64, 64), 1)
+    pick = jnp.where(channel == 4 * (to & 15) + (to >> 4), 1.0, 0.0).astype(jnp.bfloat16)
+    image[...] = dot(pick, latents, 1, 1).astype(jnp.bfloat16)
+    edge = remote(
+        image.at[pl.ds(pl.multiple_of(32 * other, 32), 32)], halo, halo_sem.at[0], halo_sem.at[1], (p, other, b)
+    )
+    edge.start()
+    for half in range(2):
+        lanes = slice(half * 128, half * 128 + 128)
+        strip[16:32, lanes] = image[half * 16 : half * 16 + 16, :]
+        strip[32:48, lanes] = image[32 + half * 16 : 32 + half * 16 + 16, :]
+    edge.wait_recv()
+    for half in range(2):
+        lanes = slice(half * 128, half * 128 + 128)
+        beside = halo[half * 16 : half * 16 + 16, :].astype(jnp.float32)
+        strip[0:16, lanes] = jnp.where(s == 1, beside, 0.0).astype(jnp.bfloat16)
+        strip[48:64, lanes] = jnp.where(s == 0, beside, 0.0).astype(jnp.bfloat16)
+    shifted = dot(strip[...], spread[...])
+    for e in range(3):
+        for f in range(4):
+            lanes = slice(e * 256 + f * 64, e * 256 + f * 64 + 64)
+            block = jnp.concatenate([shifted[0:48, lanes], shifted[16:64, lanes]], axis=1).astype(jnp.bfloat16)
+            for t in range(3):
+                for frame in range(4):
+                    if max(frame + t - 2, 0) == f:
+                        for y in range(3):
+                            at = (t * 9 + y * 3 + e) * 16
+                            columns[at : at + 16, frame * 128 : frame * 128 + 128] = block[y * 16 : y * 16 + 16]
+    for f in range(4):
+        decoded = dot(conv_w[...], columns[:, f * 128 : f * 128 + 128], 0, 0)
+        out[f] = (decoded + bias[...]).astype(jnp.bfloat16)
+
+    for db in (1, 3, 2):
+        row_copy(db, b).wait_send()
+        res_copy(db, b).wait_send()
+        noisy_copy(db, b).wait_send()
+        for dp in (1, 2, 3):
+            share_copy(froms[db], dp, p).wait_send()
+    for g in range(4):
+        for db, ds in pairs:
+            qkv_copy(g, db, ds, b, s).wait_send()
+    for c in range(4):
+        part_copy(c).wait_send()
+    edge.wait_send()
+
+
+def fused(
+    projections,
+    residual,
+    out_proj,
+    modulation,
+    final_weight,
+    final_bias,
+    noisy_latents,
+    step_size,
+    conv_weight,
+    conv_bias,
+):
+    anywhere = pl.BlockSpec(memory_space=pl.ANY)
+    vmem = pl.BlockSpec(memory_space=pltpu.VMEM)
+    smem = pl.BlockSpec(memory_space=pltpu.SMEM)
+    half, full = jnp.bfloat16, jnp.float32
+    dma = pltpu.SemaphoreType.DMA
+    decoded = pl.pallas_call(
+        fused_kernel,
+        out_shape=jax.ShapeDtypeStruct((4, 512, 128), half),
+        in_specs=[anywhere] * 4 + [vmem] * 3 + [smem] + [vmem] * 2,
+        out_specs=vmem,
+        scratch_shapes=[
+            pltpu.VMEM((3, 4, 2, 4, 2, 32, 128), half),
+            pltpu.VMEM((16, 4, 32, 128), half),
+            pltpu.VMEM((4, 32, 64), full),
+            pltpu.VMEM((1024, 2048), half),
+            pltpu.VMEM((2, 128, 1024), half),
+            pltpu.VMEM((128, 2048), half),
+            pltpu.VMEM((128, 2048), half),
+            pltpu.VMEM((128, 2048), full),
+            pltpu.VMEM((128, 2048), half),
+            pltpu.VMEM((64, 128), half),
+            pltpu.VMEM((32, 128), half),
+            pltpu.VMEM((64, 256), half),
+            pltpu.VMEM((256, 768), half),
+            pltpu.VMEM((432, 512), half),
+            pltpu.VMEM((512, 128), full),
+            pltpu.VMEM((8, 2048), full),
+            dma((4, 4, 2)),
+            dma((4, 4, 2)),
+            dma((4,)),
+            dma((4,)),
+            dma((4,)),
+            dma((4,)),
+            dma((4,)),
+            dma((4,)),
+            dma((4, 4)),
+            dma((4, 4)),
+            dma((4,)),
+            dma((4,)),
+            dma((2,)),
+            dma((10,)),
+        ],
+        compiler_params=pltpu.CompilerParams(
+            collective_id=0, has_side_effects=True, vmem_limit_bytes=40 * 1024 * 1024
+        ),
+    )(
+        projections.reshape(3, 4, 4, 2, 2, 32, 128),
+        residual.reshape(4, 16, 32, 128),
+        out_proj.reshape(2, 4, 64, 2048),
+        noisy_latents.reshape(4, 32, 64),
+        modulation,
+        final_weight,
+        final_bias.reshape(1, 64),
+        step_size,
+        conv_weight.reshape(432, 512),
+        conv_bias.reshape(1, 512),
+    )
+    return decoded[None]
+
+
 def solution(mesh):
     return jax.shard_map(
-        body,
+        fused if fits(mesh) else body,
         mesh=mesh,
         in_specs=(
             P(None, None, None, "blk", "seq", None),

time: 289 us -> 99.7 us (0.34)
  waiting for transfers between devices: 205 us -> 0 us
  Pallas kernels: 0 us -> 88 us
  local copies, waits for them, and re-layouts: 31.1 us -> 10.8 us
  starting transfers between devices: 19.5 us -> 0 us
  between operations: 13.8 us -> 0.03 us
  matrix products: 9.38 us -> 0 us
  blocking collectives: 7.96 us -> 0 us
    all_gather x2 -> x0, waiting for transfers between devices: 148 us -> none  [the longest x1 76.8 us: body(): kv_frames = lax.all_gather(pair_major[1:], 'blk', axis=3, tiled=True)]
    pallas_call x0 -> x1, Pallas kernels: none -> 88 us  [fused(): pl.pallas_call(fused_kernel, out_shape=jax.ShapeDtypeStruct((4, 512, 128)...]
    all_to_all x3 -> x0, waiting for transfers between devices: 54.9 us -> none  [the longest x1 47.6 us: body(): lax.all_to_all(kv_frames, 'seq', split_axis=1, concat_axis=4, tiled=True)]
    all_to_all x3 -> x0, starting transfers between devices: 13.6 us -> none  [the longest x1 5.95 us: body(): lax.all_to_all(kv_frames, 'seq', split_axis=1, concat_axis=4, tiled=True)]
    dot_general x1 -> x0, local copies, waits for them, and re-layouts: 11.8 us -> none  [body(): jnp.dot(token_rows, lax.all_gather(out_proj, 'blk', axis=0, tiled=True),...]
    unnamed x45 -> x20, local copies, waits for them, and re-layouts: 1.14 us -> 10.8 us
    dot_general x5 -> x0, matrix products: 9.38 us -> none  [the longest x1 6.41 us: body(): jnp.dot(token_rows, lax.all_gather(out_proj, 'blk', axis=0, tiled=True),...]
    slice x7 -> x0, local copies, waits for them, and re-layouts: 8.4 us -> none  [the longest x2 3.6 us: body(): received[1][0, 0]]
  transfers between devices with their start and end apart: 7 -> 0, of which waited for: 5 -> 0; matrix products, arithmetic and copies ran while one was open for 6% -> 0% of each run, Pallas kernels for 0% -> 0%
where the time goes in v1:
time: 99.7 us; the launch traced here: 98.8 us
  Pallas kernels  88 us (88%)
  local copies, waits for them, and re-layouts  10.8 us (11%)
    pallas_call x1, Pallas kernels, fused(): pl.pallas_call(fused_kernel, out_shape=jax.ShapeDtypeStruct((4, 512, 128)...  88 us
    unnamed x20, local copies, waits for them, and re-layouts  10.8 us

profile of v1, /device:TPU:0, one launch (start us, length us, event | category | flops | bytes accessed | tf_op | source)
XLA Modules:
  0.0 98.8 jit_solution(8827344753286099335)
XLA Ops:
  0.0 1.2 %copy.11.final_w = bf16[2048,64]{1,0:T(8,128)(2,1)S(1)} copy(bf16[2048,64]{0,1:T(8,128)(2,1)} %param.14) | data formatting | bytes 524288 | tf_op args[4]
  1.2 0.0 copy-start
  1.2 1.6 %copy-done = bf16[512,2048]{1,0:T(8,128)(2,1)S(1)} copy-done((bf16[512,2048]{1,0:T(8,128)(2,1)S(1)}, bf16[512,2048]{1,0:T(8,128)(2,1)}, u32[]{:S(2)}) %copy-start) | copy-done | bytes 2097176
  2.8 0.0 copy-start.1
  2.8 1.4 %copy-done.1 = bf16[3,4,16,1,32,128]{5,4,3,2,1,0:T(8,128)(2,1)S(1)} copy-done((bf16[3,4,16,1,32,128]{5,4,3,2,1,0:T(8,128)(2,1)S(1)}, bf16[3,4,16,1,32,128]{5,4,3,2,1,0:T(8,128)(2,1)}, u32[]{:S(2)}) %copy-start.1) | copy-done | bytes 1572888
  4.2 0.0 copy-start.2
  4.2 1.0 %copy-done.2 = bf16[4,16,1,32,128]{4,3,2,1,0:T(8,128)(2,1)S(1)} copy-done((bf16[4,16,1,32,128]{4,3,2,1,0:T(8,128)(2,1)S(1)}, bf16[4,16,1,32,128]{4,3,2,1,0:T(8,128)(2,1)}, u32[]{:S(2)}) %copy-start.2) | copy-done | bytes 524312
  5.3 0.0 copy-start.3
  5.3 1.0 %copy-done.3 = bf16[3,3,3,16,512]{4,3,2,1,0:T(8,128)(2,1)S(1)} copy-done((bf16[3,3,3,16,512]{4,3,2,1,0:T(8,128)(2,1)S(1)}, bf16[3,3,3,16,512]{4,3,2,1,0:T(8,128)(2,1)}, u32[]{:S(2)}) %copy-start.3) | copy-done | bytes 442392
  6.3 0.0 copy-start.4
  6.3 0.9 copy-done.4
  7.2 0.0 copy-start.5
  7.2 0.8 copy-done.5
  8.0 0.0 copy-start.6
  8.0 0.7 copy-done.6
  8.7 0.0 copy-start.7
  8.7 0.7 copy-done.7
  9.4 0.0 copy-start.8
  9.4 0.7 copy-done.8
  10.0 88.0 %shard_map.100 = bf16[4,512,128]{2,1,0:T(8,128)(2,1)S(1)} custom-call(bf16[3,4,4,2,2,32,128]{6,5,4,3,2,1,0:T(8,128)(2,1)S(1)} %bitcast.10, bf16[4,16,32,128]{3,2,1,0:T(8,128)(2,1)S(1)} %bitcast.11, bf16[2,4,64,2048]{3,2,1,0:T(8,128)(2,1)S(1)} %bitcast.9, f32[4,32,64]{2,1,0:T(8,128)S(1)} %bitcast.13, f32[3,4,2048]{2,1,0:T(4,128)S(1)} %copy-done.4, ...), custom_call_target="tpu_custom_call" | custom-call | tf_op jit(solution)/shard_map/pallas_call | solution.py:445
  98.0 0.8 copy.13
Async XLA Ops:
  1.2 1.6 %copy-start = (bf16[512,2048]{1,0:T(8,128)(2,1)S(1)}, bf16[512,2048]{1,0:T(8,128)(2,1)}, u32[]{:S(2)}) copy-start(bf16[512,2048]{1,0:T(8,128)(2,1)} %param.12) | copy-start | bytes 6291460
  2.8 1.4 %copy-start.1 = (bf16[3,4,16,1,32,128]{5,4,3,2,1,0:T(8,128)(2,1)S(1)}, bf16[3,4,16,1,32,128]{5,4,3,2,1,0:T(8,128)(2,1)}, u32[]{:S(2)}) copy-start(bf16[3,4,16,1,32,128]{5,4,3,2,1,0:T(8,128)(2,1)} %param.10) | copy-start | bytes 4718596
  4.2 1.0 %copy-start.2 = (bf16[4,16,1,32,128]{4,3,2,1,0:T(8,128)(2,1)S(1)}, bf16[4,16,1,32,128]{4,3,2,1,0:T(8,128)(2,1)}, u32[]{:S(2)}) copy-start(bf16[4,16,1,32,128]{4,3,2,1,0:T(8,128)(2,1)} %param.11) | copy-start | bytes 1572868
  5.3 1.0 %copy-start.3 = (bf16[3,3,3,16,512]{4,3,2,1,0:T(8,128)(2,1)S(1)}, bf16[3,3,3,16,512]{4,3,2,1,0:T(8,128)(2,1)}, u32[]{:S(2)}) copy-start(bf16[3,3,3,16,512]{4,3,2,1,0:T(8,128)(2,1)} %param.18) | copy-start | bytes 1327108
  6.3 0.9 copy-start.4
  7.2 0.8 copy-start.5
  8.0 0.7 copy-start.6
  8.7 0.7 copy-start.7
  9.4 0.7 copy-start.8

commit v2 on v1

--- a/solution.py
+++ b/solution.py
@@ -187,29 +187,33 @@
     res_in,
     out_w,
     noisy_in,
-    mod,
-    final_w,
-    final_b,
+    mod_in,
+    final_in,
+    final_b_in,
+    conv_in,
+    conv_b_in,
     step,
-    conv_w,
-    conv_b,
     out,
     qkv,
     res,
     noisy,
     rows,
     att,
-    part_out,
-    part_in,
-    mixed,
-    normal,
-    image,
-    halo,
+    projected,
+    centred,
+    summary_out,
+    summary_in,
     strip,
     spread,
     columns,
     bias,
     factors,
+    mod,
+    final_w,
+    final_b,
+    conv_w,
+    conv_b,
+    conv_t,
     qkv_send,
     qkv_recv,
     res_send,
@@ -218,11 +222,12 @@
     noisy_recv,
     row_send,
     row_recv,
+    forward_send,
     share_send,
     share_recv,
-    part_send,
-    part_recv,
-    halo_sem,
+    att_send,
+    att_recv,
+    summary_sem,
     local_sem,
 ):
     p, s, b = lax.axis_index("prompt"), lax.axis_index("seq"), lax.axis_index("blk")
@@ -251,11 +256,22 @@
             device_id_type=pl.DeviceIdType.MESH,
         )
 
+    near = b + 1 - 2 * lax.rem(b, 2)
+    inner = 2 - b // 2
+    outer = 3 * (1 - b // 2)
+
     def row_slot(group, quarter):
-        return rows.at[pl.ds(pl.multiple_of(group * 256 + quarter * 64, 64), 64)]
-
-    def row_copy(db, source):
-        return remote(out_w.at[s, p], row_slot(source, p), row_send.at[db], row_recv.at[source], (p, s, blks[db]))
+        return rows.at[pl.ds(pl.multiple_of(group * 512 + quarter * 128, 128), 128)]
+
+    def own_rows(quarter):
+        return out_w.at[quarter, :, pl.ds(pl.multiple_of(s * 1024, 1024), 1024)]
+
+    def row_copy(k, target, source):
+        return remote(own_rows(p), row_slot(source, p), row_send.at[k], row_recv.at[source], (p, s, target))
+
+    def forward_copy(k, source):
+        slot = row_slot(source, p)
+        return remote(slot, slot, forward_send.at[k], row_recv.at[source], (p, s, near))
 
     def share_copy(group, dp, source):
         return remote(
@@ -275,45 +291,93 @@
             (p, seqs[ds], blks[db]),
         )
 
-    def res_copy(db, frame):
-        return remote(res_in.at[blks[db]], res.at[:, frame], res_send.at[db], res_recv.at[frame], (p, s, blks[db]))
-
-    def noisy_copy(db, frame):
-        return remote(noisy_in.at[blks[db]], noisy.at[frame], noisy_send.at[db], noisy_recv.at[frame], (p, s, blks[db]))
-
-    for db in (2, 1, 3):
-        row_copy(db, b).start()
+    def res_copy(db, ds, frame, row):
+        return remote(
+            res_in.at[blks[db], seqs[ds]],
+            res.at[:, frame, row],
+            res_send.at[db, ds],
+            res_recv.at[frame, row],
+            (p, seqs[ds], blks[db]),
+        )
+
+    def noisy_copy(db, ds, frame, row):
+        return remote(
+            noisy_in.at[blks[db]],
+            noisy.at[frame, row],
+            noisy_send.at[db, ds],
+            noisy_recv.at[frame, row],
+            (p, seqs[ds], blks[db]),
+        )
+
+    row_copy(0, inner, b).start()
+    row_copy(1, near, b).start()
     for g in range(4):
         for db, ds in pairs:
             qkv_copy(g, db, ds, b, s).start()
-    for db in (2, 1, 3):
-        noisy_copy(db, b).start()
-        res_copy(db, b).start()
+    for db, ds in pairs:
+        noisy_copy(db, ds, b, s).start()
+        res_copy(db, ds, b, s).start()
     own = [
         pltpu.make_async_copy(proj.at[:, b, g, s], qkv.at[:, g, :, b, s], local_sem.at[g]) for g in range(4)
     ]
-    own.append(pltpu.make_async_copy(res_in.at[b], res.at[:, b], local_sem.at[4]))
-    own.append(pltpu.make_async_copy(noisy_in.at[b], noisy.at[b], local_sem.at[5]))
+    own.append(pltpu.make_async_copy(res_in.at[b, s], res.at[:, b, s], local_sem.at[4]))
+    own.append(pltpu.make_async_copy(noisy_in.at[b], noisy.at[b, s], local_sem.at[5]))
     for quarter in range(4):
-        own.append(pltpu.make_async_copy(out_w.at[s, quarter], row_slot(b, quarter), local_sem.at[6 + quarter]))
+        own.append(pltpu.make_async_copy(own_rows(quarter), row_slot(b, quarter), local_sem.at[6 + quarter]))
+    tables = ((mod_in, mod), (final_in, final_w), (final_b_in, final_b), (conv_in, conv_w), (conv_b_in, conv_b))
+    for k, (src, dst) in enumerate(tables):
+        own.append(pltpu.make_async_copy(src, dst, local_sem.at[10 + k]))
     for copy in own:
         copy.start()
 
     for half in range(2):
-        at_row = lax.broadcasted_iota(jnp.int32, (128, 768), 0)
-        at_col = lax.broadcasted_iota(jnp.int32, (128, 768), 1)
-        same = (at_row >> 5) == ((at_col >> 6) & 3)
+        at_row = lax.broadcasted_iota(jnp.int32, (256, 768), 0)
+        at_col = lax.broadcasted_iota(jnp.int32, (256, 768), 1)
+        same = (at_row >> 6) == ((at_col >> 6) & 3)
         place = (at_col & 63) == 2 * (at_row & 31) + (half + 1) - (at_col >> 8)
-        spread[half * 128 : half * 128 + 128, :] = jnp.where(same & place, 1.0, 0.0).astype(jnp.bfloat16)
+        spread[half * 256 : half * 256 + 256, :] = jnp.where(same & place, 1.0, 0.0).astype(jnp.bfloat16)
+    for copy in own[10:]:
+        copy.wait()
     for k in range(3):
         video = lax.broadcasted_iota(jnp.int32, (4, 2048), 0)
         factors[k : k + 1, :] = jnp.sum(jnp.where(video == b, mod[k], 0.0), axis=0, keepdims=True)
     bias[...] = jnp.broadcast_to(conv_b[...], (128, 512)).T
 
-    for db in (1, 3, 2):
-        row_copy(db, froms[db]).wait_recv()
+    conv_t[...] = conv_w[...].T
+
+    def split(value):
+        high = value.astype(jnp.bfloat16)
+        return high.astype(jnp.float32), value - high.astype(jnp.float32)
+
+    row = lax.broadcasted_iota(jnp.int32, (8, 1024), 0)
+    tilts = []
+    moved = final_b[...]
+    for half in range(2):
+        lanes = slice(half * 1024, half * 1024 + 1024)
+        high, low = split(1.0 + factors[1:2, lanes])
+        shift_high, shift_low = split(factors[0:1, lanes])
+        parts = jnp.where(row == 0, high, 0.0) + jnp.where(row == 1, low, 0.0)
+        parts = parts + jnp.where(row == 2, shift_high, 0.0) + jnp.where(row == 3, shift_low, 0.0)
+        sums = dot(parts.astype(jnp.bfloat16), final_w[:, lanes], 1, 1)
+        tilts.append(sums[0:1] + sums[1:2])
+        moved = moved + sums[2:3] + sums[3:4]
+    tilt_mine = jnp.where(s == 0, tilts[0], tilts[1])
+    tilt_other = jnp.where(s == 0, tilts[1], tilts[0])
+
+    for k, source in enumerate((near, inner, outer)):
+        row_copy(0, near, source).wait_recv()
+        if k > 0:
+
+            @pl.when(lax.rem(b, 3) != 0)
+            def _(k=k, source=source):
+                forward_copy(k - 1, source).start()
+
         for dp in (1, 2, 3):
-            share_copy(froms[db], dp, p).start()
+            share_copy(source, dp, p).start()
+
+    def att_copy(g, side):
+        cols = att.at[:, pl.ds(pl.multiple_of((4 * g + 2 * side) * 128, 256), 256)]
+        return remote(cols, cols, att_send.at[g], att_recv.at[g], (p, other, b))
 
     scale = 128 ** (-0.5)
     for g in range(4):
@@ -328,74 +392,74 @@
             weights = jnp.exp(scores - jnp.max(scores, axis=1, keepdims=True))
             totals = jnp.sum(weights, axis=1, keepdims=True)
             result = (dot(weights.astype(jnp.bfloat16), value) / totals).astype(jnp.bfloat16)
-            at = (g * 2 + k) * 128
-            for f in range(4):
-                for i in range(2):
-                    att[i, f * 32 : f * 32 + 32, at : at + 128] = result[f * 64 + i * 32 : f * 64 + i * 32 + 32]
-
-    for quarter in range(4):
-        own[6 + quarter].wait()
-    for db in (1, 3, 2):
-        for dp in (1, 2, 3):
-            share_copy(froms[db], dp, prompt_froms[dp]).wait_recv()
-
-    def part_copy(c):
-        cols = pl.ds(c * 512, 512)
-        return remote(part_out.at[:, cols], part_in.at[:, cols], part_send.at[c], part_recv.at[c], (p, other, b))
-
-    for c in range(4):
-        part_out[:, c * 512 : c * 512 + 512] = dot(att[other], rows[:, c * 512 : c * 512 + 512]).astype(jnp.bfloat16)
-        part_copy(c).start()
+            att[:, pl.ds(pl.multiple_of((4 * g + 2 * s + k) * 128, 128), 128)] = result
+        att_copy(g, s).start()
+        if g == 2:
+            for quarter in range(4):
+                own[6 + quarter].wait()
+            for source in (near, inner, outer):
+                for dp in (1, 2, 3):
+                    share_copy(source, dp, prompt_froms[dp]).wait_recv()
+            for done in range(3):
+                att_copy(done, other).wait_recv()
+            for n in range(2):
+                lanes = slice(n * 512, n * 512 + 512)
+                projected[:, lanes] = dot(att[:, 0:1536], rows[0:1536, lanes])
+
     own[4].wait()
-    for db in (1, 3, 2):
-        res_copy(db, froms[db]).wait_recv()
-
-    total = jnp.zeros((128, 128), jnp.float32)
-    for c in range(4):
-        mine = dot(att[s], rows[:, c * 512 : c * 512 + 512])
-        part_copy(c).wait_recv()
+    for db, ds in pairs:
+        res_copy(db, ds, froms[db], seqs[ds]).wait_recv()
+    att_copy(3, other).wait_recv()
+    total = jnp.zeros((256, 128), jnp.float32)
+    for n in range(2):
+        last = dot(att[:, 1536:2048], rows[1536:2048, n * 512 : n * 512 + 512])
         for k in range(4):
-            h = c * 4 + k
-            at = h * 128
-            projected = mine[:, k * 128 : k * 128 + 128] + part_in[:, at : at + 128].astype(jnp.float32)
-            value = res[h].reshape(128, 128).astype(jnp.float32) + factors[2:3, at : at + 128] * projected
-            mixed[:, at : at + 128] = value
+            h = n * 4 + k
+            lanes = slice(h * 128, h * 128 + 128)
+            value = projected[:, lanes] + last[:, k * 128 : k * 128 + 128]
+            gate = jnp.where(s == 0, factors[2:3, lanes], factors[2:3, 1024 + h * 128 : 1152 + h * 128])
+            value = res[h].reshape(256, 128).astype(jnp.float32) + gate * value
+            projected[:, lanes] = value
             total = total + value
-    center = jnp.sum(total, axis=1, keepdims=True) * (1.0 / 2048)
-    total = jnp.zeros((128, 128), jnp.float32)
-    for h in range(16):
-        total = total + jnp.square(mixed[:, h * 128 : h * 128 + 128] - center)
-    inverse = lax.rsqrt(jnp.sum(total, axis=1, keepdims=True) * (1.0 / 2048) + 1e-06)
-    for h in range(16):
-        at = h * 128
-        normed = (mixed[:, at : at + 128] - center) * inverse
-        normal[:, at : at + 128] = (
-            normed * (1.0 + factors[1:2, at : at + 128]) + factors[0:1, at : at + 128]
-        ).astype(jnp.bfloat16)
-    prediction = dot(normal[...], final_w[...]) + final_b[...]
+    center = jnp.sum(total, axis=1, keepdims=True) * (1.0 / 1024)
+    total = jnp.zeros((256, 128), jnp.float32)
+    for h in range(8):
+        lanes = slice(h * 128, h * 128 + 128)
+        away = projected[:, lanes] - center
+        total = total + jnp.square(away)
+        gain = jnp.where(s == 0, factors[1:2, lanes], factors[1:2, 1024 + h * 128 : 1152 + h * 128])
+        centred[:, lanes] = (away * (1.0 + gain)).astype(jnp.bfloat16)
+    squares = jnp.sum(total, axis=1, keepdims=True)
+    weighted = dot(centred[...], final_w[:, pl.ds(pl.multiple_of(s * 1024, 1024), 1024)], 1, 1)
+    summary_out[:, 0:64] = weighted
+    lane = lax.broadcasted_iota(jnp.int32, (256, 64), 1)
+    summary_out[:, 64:128] = jnp.where(lane == 0, center, jnp.where(lane == 1, squares, 0.0))
+    summary = remote(summary_out, summary_in, summary_sem.at[0], summary_sem.at[1], (p, other, b))
+    summary.start()
     own[5].wait()
-    for db in (1, 3, 2):
-        noisy_copy(db, froms[db]).wait_recv()
-    latents = ((noisy[...].reshape(128, 64) + step[b] * prediction) / 0.476986).astype(jnp.bfloat16)
+    for db, ds in pairs:
+        noisy_copy(db, ds, froms[db], seqs[ds]).wait_recv()
+    start = noisy[...].reshape(256, 64)
+    summary.wait_recv()
+    center_other = summary_in[:, 64:65]
+    squares = squares + summary_in[:, 65:66]
+    apart = (center - center_other) * 0.5
+    inverse = lax.rsqrt(squares * (1.0 / 2048) + jnp.square(apart) + 1e-06)
+    weighted = weighted + summary_in[:, 0:64] + apart * (tilt_mine - tilt_other)
+    prediction = inverse * weighted + moved
+    latents = ((start + step[b] * prediction) / 0.476986).astype(jnp.bfloat16)
 
     to = lax.broadcasted_iota(jnp.int32, (64, 64), 0)
     channel = lax.broadcasted_iota(jnp.int32, (64, 64), 1)
     pick = jnp.where(channel == 4 * (to & 15) + (to >> 4), 1.0, 0.0).astype(jnp.bfloat16)
-    image[...] = dot(pick, latents, 1, 1).astype(jnp.bfloat16)
-    edge = remote(
-        image.at[pl.ds(pl.multiple_of(32 * other, 32), 32)], halo, halo_sem.at[0], halo_sem.at[1], (p, other, b)
-    )
-    edge.start()
-    for half in range(2):
-        lanes = slice(half * 128, half * 128 + 128)
-        strip[16:32, lanes] = image[half * 16 : half * 16 + 16, :]
-        strip[32:48, lanes] = image[32 + half * 16 : 32 + half * 16 + 16, :]
-    edge.wait_recv()
-    for half in range(2):
-        lanes = slice(half * 128, half * 128 + 128)
-        beside = halo[half * 16 : half * 16 + 16, :].astype(jnp.float32)
-        strip[0:16, lanes] = jnp.where(s == 1, beside, 0.0).astype(jnp.bfloat16)
-        strip[48:64, lanes] = jnp.where(s == 0, beside, 0.0).astype(jnp.bfloat16)
+    image = dot(pick, latents, 1, 1)
+    row_of = (lax.broadcasted_iota(jnp.int32, (16, 256), 1) >> 5) & 1
+    for r in range(4):
+        here = row_of == s + (r + 1) // 2 - 1
+        for half in range(2):
+            at = (1 - r % 2) * 32 + half * 16
+            kept = jnp.where(here, image[at : at + 16], 0.0).astype(jnp.bfloat16)
+            strip[r * 16 : r * 16 + 16, half * 256 : half * 256 + 256] = kept
     shifted = dot(strip[...], spread[...])
     for e in range(3):
         for f in range(4):
@@ -408,21 +472,29 @@
                             at = (t * 9 + y * 3 + e) * 16
                             columns[at : at + 16, frame * 128 : frame * 128 + 128] = block[y * 16 : y * 16 + 16]
     for f in range(4):
-        decoded = dot(conv_w[...], columns[:, f * 128 : f * 128 + 128], 0, 0)
+        decoded = dot(conv_t[...], columns[:, f * 128 : f * 128 + 128])
         out[f] = (decoded + bias[...]).astype(jnp.bfloat16)
 
-    for db in (1, 3, 2):
-        row_copy(db, b).wait_send()
-        res_copy(db, b).wait_send()
-        noisy_copy(db, b).wait_send()
+    for k, source in enumerate((near, inner, outer)):
+        if k < 2:
+            row_copy(k, near, b).wait_send()
+        else:
+
+            @pl.when(lax.rem(b, 3) != 0)
+            def _():
+                forward_copy(0, inner).wait_send()
+                forward_copy(1, outer).wait_send()
+
         for dp in (1, 2, 3):
-            share_copy(froms[db], dp, p).wait_send()
+            share_copy(source, dp, p).wait_send()
+    for db, ds in pairs:
+        res_copy(db, ds, b, s).wait_send()
+        noisy_copy(db, ds, b, s).wait_send()
+        for g in range(4):
+            qkv_copy(g, db, ds, b, s).wait_send()
     for g in range(4):
-        for db, ds in pairs:
-            qkv_copy(g, db, ds, b, s).wait_send()
-    for c in range(4):
-        part_copy(c).wait_send()
-    edge.wait_send()
+        att_copy(g, s).wait_send()
+    summary.wait_send()
 
 
 def fused(
@@ -445,54 +517,59 @@
     decoded = pl.pallas_call(
         fused_kernel,
         out_shape=jax.ShapeDtypeStruct((4, 512, 128), half),
-        in_specs=[anywhere] * 4 + [vmem] * 3 + [smem] + [vmem] * 2,
+        in_specs=[anywhere] * 9 + [smem],
         out_specs=vmem,
         scratch_shapes=[
             pltpu.VMEM((3, 4, 2, 4, 2, 32, 128), half),
-            pltpu.VMEM((16, 4, 32, 128), half),
-            pltpu.VMEM((4, 32, 64), full),
-            pltpu.VMEM((1024, 2048), half),
-            pltpu.VMEM((2, 128, 1024), half),
-            pltpu.VMEM((128, 2048), half),
-            pltpu.VMEM((128, 2048), half),
-            pltpu.VMEM((128, 2048), full),
-            pltpu.VMEM((128, 2048), half),
-            pltpu.VMEM((64, 128), half),
-            pltpu.VMEM((32, 128), half),
-            pltpu.VMEM((64, 256), half),
-            pltpu.VMEM((256, 768), half),
+            pltpu.VMEM((8, 4, 2, 32, 128), half),
+            pltpu.VMEM((4, 2, 32, 64), full),
+            pltpu.VMEM((2048, 1024), half),
+            pltpu.VMEM((256, 2048), half),
+            pltpu.VMEM((256, 1024), full),
+            pltpu.VMEM((256, 1024), half),
+            pltpu.VMEM((256, 128), full),
+            pltpu.VMEM((256, 128), full),
+            pltpu.VMEM((64, 512), half),
+            pltpu.VMEM((512, 768), half),
             pltpu.VMEM((432, 512), half),
             pltpu.VMEM((512, 128), full),
             pltpu.VMEM((8, 2048), full),
+            pltpu.VMEM((3, 4, 2048), full),
+            pltpu.VMEM((64, 2048), half),
+            pltpu.VMEM((1, 64), full),
+            pltpu.VMEM((432, 512), half),
+            pltpu.VMEM((1, 512), full),
+            pltpu.VMEM((512, 432), half),
             dma((4, 4, 2)),
             dma((4, 4, 2)),
+            dma((4, 2)),
+            dma((4, 2)),
+            dma((4, 2)),
+            dma((4, 2)),
+            dma((2,)),
             dma((4,)),
-            dma((4,)),
-            dma((4,)),
-            dma((4,)),
-            dma((4,)),
-            dma((4,)),
+            dma((2,)),
             dma((4, 4)),
             dma((4, 4)),
             dma((4,)),
             dma((4,)),
             dma((2,)),
-            dma((10,)),
+            dma((15,)),
         ],
         compiler_params=pltpu.CompilerParams(
-            collective_id=0, has_side_effects=True, vmem_limit_bytes=40 * 1024 * 1024
+            collective_id=0, has_side_effects=True, vmem_limit_bytes=60 * 1024 * 1024
         ),
     )(
         projections.reshape(3, 4, 4, 2, 2, 32, 128),
-        residual.reshape(4, 16, 32, 128),
-        out_proj.reshape(2, 4, 64, 2048),
+        residual.reshape(4, 2, 8, 32, 128),
+        out_proj.reshape(4, 128, 2048),
         noisy_latents.reshape(4, 32, 64),
         modulation,
-        final_weight,
+        final_weight.T,
         final_bias.reshape(1, 64),
-        step_size,
         conv_weight.reshape(432, 512),
         conv_bias.reshape(1, 512),
+        step_size,
     )
     return decoded[None]
 

time: 99.7 us -> 82.2 us (0.82)
  local copies, waits for them, and re-layouts: 10.8 us -> 1.87 us
  Pallas kernels: 88 us -> 80.1 us
    unnamed x20 -> x1, local copies, waits for them, and re-layouts: 10.8 us -> 1.87 us
    pallas_call x1, Pallas kernels: 88 us -> 80.1 us  [fused(): pl.pallas_call(fused_kernel, out_shape=jax.ShapeDtypeStruct((4, 512, 128)...]
where the time goes in v2:
time: 82.2 us; the launch traced here: 82 us
  Pallas kernels  80.1 us (97%)
  local copies, waits for them, and re-layouts  1.87 us (2%)
    pallas_call x1, Pallas kernels, fused(): pl.pallas_call(fused_kernel, out_shape=jax.ShapeDtypeStruct((4, 512, 128)...  80.1 us
    unnamed x1, local copies, waits for them, and re-layouts  1.87 us

profile of v2, /device:TPU:0, one launch (start us, length us, event | category | flops | bytes accessed | tf_op | source)
XLA Modules:
  0.0 82.0 jit_solution(6245859609559954718)
XLA Ops:
  0.0 80.1 %shard_map.100 = bf16[4,512,128]{2,1,0:T(8,128)(2,1)} custom-call(bf16[3,4,4,2,2,32,128]{6,5,4,3,2,1,0:T(8,128)(2,1)} %bitcast.11, bf16[4,2,8,32,128]{4,3,2,1,0:T(8,128)(2,1)} %bitcast.12, bf16[4,128,2048]{2,1,0:T(8,128)(2,1)} %bitcast.9, f32[4,32,64]{2,1,0:T(8,128)} %bitcast.15, f32[3,4,2048]{2,1,0:T(4,128)} %mod_in.1, bf16[64,2048]{1,0:T(8,128)(2,1)} %bitcast.14, ...), custom_call_target="tpu_custom_call" | custom-call | tf_op jit(solution)/shard_map/pallas_call | solution.py:517
  80.1 1.9 %copy.12 = bf16[1,4,512,128]{3,2,1,0:T(8,128)(2,1)} copy(bf16[1,4,512,128]{3,2,1,0:T(8,128)(2,1)} %bitcast.10) | data formatting | bytes 1048576

commit v3 on v2

--- a/solution.py
+++ b/solution.py
@@ -311,12 +311,8 @@
 
     row_copy(0, inner, b).start()
     row_copy(1, near, b).start()
-    for g in range(4):
-        for db, ds in pairs:
-            qkv_copy(g, db, ds, b, s).start()
     for db, ds in pairs:
-        noisy_copy(db, ds, b, s).start()
-        res_copy(db, ds, b, s).start()
+        qkv_copy(0, db, ds, b, s).start()
     own = [
         pltpu.make_async_copy(proj.at[:, b, g, s], qkv.at[:, g, :, b, s], local_sem.at[g]) for g in range(4)
     ]
@@ -329,6 +325,27 @@
         own.append(pltpu.make_async_copy(src, dst, local_sem.at[10 + k]))
     for copy in own:
         copy.start()
+
+    def share(source):
+        for dp in (1, 2, 3):
+            share_copy(source, dp, p).start()
+
+    row_copy(0, near, near).wait_recv()
+    share(near)
+
+    @pl.when(lax.rem(b, 3) != 0)
+    def _():
+        for k, source in enumerate((inner, outer)):
+            row_copy(0, near, source).wait_recv()
+            forward_copy(k, source).start()
+            share(source)
+
+    for g in range(1, 4):
+        for db, ds in pairs:
+            qkv_copy(g, db, ds, b, s).start()
+    for db, ds in pairs:
+        noisy_copy(db, ds, b, s).start()
+        res_copy(db, ds, b, s).start()
 
     for half in range(2):
         at_row = lax.broadcasted_iota(jnp.int32, (256, 768), 0)
@@ -364,16 +381,11 @@
     tilt_mine = jnp.where(s == 0, tilts[0], tilts[1])
     tilt_other = jnp.where(s == 0, tilts[1], tilts[0])
 
-    for k, source in enumerate((near, inner, outer)):
-        row_copy(0, near, source).wait_recv()
-        if k > 0:
-
-            @pl.when(lax.rem(b, 3) != 0)
-            def _(k=k, source=source):
-                forward_copy(k - 1, source).start()
-
-        for dp in (1, 2, 3):
-            share_copy(source, dp, p).start()
+    @pl.when(lax.rem(b, 3) == 0)
+    def _():
+        for source in (inner, outer):
+            row_copy(0, near, source).wait_recv()
+            share(source)
 
     def att_copy(g, side):
         cols = att.at[:, pl.ds(pl.multiple_of((4 * g + 2 * side) * 128, 256), 256)]
@@ -394,33 +406,27 @@
             result = (dot(weights.astype(jnp.bfloat16), value) / totals).astype(jnp.bfloat16)
             att[:, pl.ds(pl.multiple_of((4 * g + 2 * s + k) * 128, 128), 128)] = result
         att_copy(g, s).start()
-        if g == 2:
-            for quarter in range(4):
-                own[6 + quarter].wait()
-            for source in (near, inner, outer):
-                for dp in (1, 2, 3):
-                    share_copy(source, dp, prompt_froms[dp]).wait_recv()
-            for done in range(3):
-                att_copy(done, other).wait_recv()
-            for n in range(2):
-                lanes = slice(n * 512, n * 512 + 512)
-                projected[:, lanes] = dot(att[:, 0:1536], rows[0:1536, lanes])
+    for quarter in range(4):
+        own[6 + quarter].wait()
+    for source in (near, inner, outer):
+        for dp in (1, 2, 3):
+            share_copy(source, dp, prompt_froms[dp]).wait_recv()
+    for done in range(4):
+        att_copy(done, other).wait_recv()
+    for n in range(2):
+        lanes = slice(n * 512, n * 512 + 512)
+        projected[:, lanes] = dot(att[...], rows[:, lanes])
 
     own[4].wait()
     for db, ds in pairs:
         res_copy(db, ds, froms[db], seqs[ds]).wait_recv()
-    att_copy(3, other).wait_recv()
     total = jnp.zeros((256, 128), jnp.float32)
-    for n in range(2):
-        last = dot(att[:, 1536:2048], rows[1536:2048, n * 512 : n * 512 + 512])
-        for k in range(4):
-            h = n * 4 + k
-            lanes = slice(h * 128, h * 128 + 128)
-            value = projected[:, lanes] + last[:, k * 128 : k * 128 + 128]
-            gate = jnp.where(s == 0, factors[2:3, lanes], factors[2:3, 1024 + h * 128 : 1152 + h * 128])
-            value = res[h].reshape(256, 128).astype(jnp.float32) + gate * value
-            projected[:, lanes] = value
-            total = total + value
+    for h in range(8):
+        lanes = slice(h * 128, h * 128 + 128)
+        gate = jnp.where(s == 0, factors[2:3, lanes], factors[2:3, 1024 + h * 128 : 1152 + h * 128])
+        value = res[h].reshape(256, 128).astype(jnp.float32) + gate * projected[:, lanes]
+        projected[:, lanes] = value
+        total = total + value
     center = jnp.sum(total, axis=1, keepdims=True) * (1.0 / 1024)
     total = jnp.zeros((256, 128), jnp.float32)
     for h in range(8):

time: 82.2 us -> 78.6 us (0.956)
  Pallas kernels: 80.1 us -> 76.5 us
    pallas_call x1, Pallas kernels: 80.1 us -> 76.5 us  [fused(): pl.pallas_call(fused_kernel, out_shape=jax.ShapeDtypeStruct((4, 512, 128)...]
where the time goes in v3:
time: 78.6 us; the launch traced here: 78.4 us
  Pallas kernels  76.5 us (97%)
  local copies, waits for them, and re-layouts  1.87 us (2%)
    pallas_call x1, Pallas kernels, fused(): pl.pallas_call(fused_kernel, out_shape=jax.ShapeDtypeStruct((4, 512, 128)...  76.5 us
    unnamed x1, local copies, waits for them, and re-layouts  1.87 us

profile of v3, /device:TPU:0, one launch (start us, length us, event | category | flops | bytes accessed | tf_op | source)
XLA Modules:
  0.0 78.4 jit_solution(6720737774337030709)
XLA Ops:
  0.0 76.5 %shard_map.100 = bf16[4,512,128]{2,1,0:T(8,128)(2,1)} custom-call(bf16[3,4,4,2,2,32,128]{6,5,4,3,2,1,0:T(8,128)(2,1)} %bitcast.11, bf16[4,2,8,32,128]{4,3,2,1,0:T(8,128)(2,1)} %bitcast.12, bf16[4,128,2048]{2,1,0:T(8,128)(2,1)} %bitcast.9, f32[4,32,64]{2,1,0:T(8,128)} %bitcast.15, f32[3,4,2048]{2,1,0:T(4,128)} %mod_in.1, bf16[64,2048]{1,0:T(8,128)(2,1)} %bitcast.14, ...), custom_call_target="tpu_custom_call" | custom-call | tf_op jit(solution)/shard_map/pallas_call | solution.py:523
  76.5 1.9 %copy.12 = bf16[1,4,512,128]{3,2,1,0:T(8,128)(2,1)} copy(bf16[1,4,512,128]{3,2,1,0:T(8,128)(2,1)} %bitcast.10) | data formatting | bytes 1048576

commit v4 on v3

--- a/solution.py
+++ b/solution.py
@@ -311,8 +311,9 @@
 
     row_copy(0, inner, b).start()
     row_copy(1, near, b).start()
-    for db, ds in pairs:
-        qkv_copy(0, db, ds, b, s).start()
+    for g in range(2):
+        for db, ds in pairs:
+            qkv_copy(g, db, ds, b, s).start()
     own = [
         pltpu.make_async_copy(proj.at[:, b, g, s], qkv.at[:, g, :, b, s], local_sem.at[g]) for g in range(4)
     ]
@@ -340,7 +341,7 @@
             forward_copy(k, source).start()
             share(source)
 
-    for g in range(1, 4):
+    for g in range(2, 4):
         for db, ds in pairs:
             qkv_copy(g, db, ds, b, s).start()
     for db, ds in pairs:

time: 78.6 us -> 77.2 us (0.982)
  Pallas kernels: 76.5 us -> 75.2 us
    pallas_call x1, Pallas kernels: 76.5 us -> 75.2 us  [fused(): pl.pallas_call(fused_kernel, out_shape=jax.ShapeDtypeStruct((4, 512, 128)...]
where the time goes in v4:
time: 77.2 us; the launch traced here: 77 us
  Pallas kernels  75.2 us (97%)
  local copies, waits for them, and re-layouts  1.87 us (2%)
    pallas_call x1, Pallas kernels, fused(): pl.pallas_call(fused_kernel, out_shape=jax.ShapeDtypeStruct((4, 512, 128)...  75.2 us
    unnamed x1, local copies, waits for them, and re-layouts  1.87 us

profile of v4, /device:TPU:0, one launch (start us, length us, event | category | flops | bytes accessed | tf_op | source)
XLA Modules:
  0.0 77.0 jit_solution(8491101603929212237)
XLA Ops:
  0.0 75.2 %shard_map.100 = bf16[4,512,128]{2,1,0:T(8,128)(2,1)} custom-call(bf16[3,4,4,2,2,32,128]{6,5,4,3,2,1,0:T(8,128)(2,1)} %bitcast.11, bf16[4,2,8,32,128]{4,3,2,1,0:T(8,128)(2,1)} %bitcast.12, bf16[4,128,2048]{2,1,0:T(8,128)(2,1)} %bitcast.9, f32[4,32,64]{2,1,0:T(8,128)} %bitcast.15, f32[3,4,2048]{2,1,0:T(4,128)} %mod_in.1, bf16[64,2048]{1,0:T(8,128)(2,1)} %bitcast.14, ...), custom_call_target="tpu_custom_call" | custom-call | tf_op jit(solution)/shard_map/pallas_call | solution.py:524
  75.2 1.9 %copy.12 = bf16[1,4,512,128]{3,2,1,0:T(8,128)(2,1)} copy(bf16[1,4,512,128]{3,2,1,0:T(8,128)(2,1)} %bitcast.10) | data formatting | bytes 1048576

commit v5 on v4

--- a/solution.py
+++ b/solution.py
@@ -341,12 +341,8 @@
             forward_copy(k, source).start()
             share(source)
 
-    for g in range(2, 4):
-        for db, ds in pairs:
-            qkv_copy(g, db, ds, b, s).start()
     for db, ds in pairs:
-        noisy_copy(db, ds, b, s).start()
-        res_copy(db, ds, b, s).start()
+        qkv_copy(2, db, ds, b, s).start()
 
     for half in range(2):
         at_row = lax.broadcasted_iota(jnp.int32, (256, 768), 0)
@@ -407,6 +403,12 @@
             result = (dot(weights.astype(jnp.bfloat16), value) / totals).astype(jnp.bfloat16)
             att[:, pl.ds(pl.multiple_of((4 * g + 2 * s + k) * 128, 128), 128)] = result
         att_copy(g, s).start()
+        for db, ds in pairs:
+            if g == 0:
+                qkv_copy(3, db, ds, b, s).start()
+            if g == 2:
+                noisy_copy(db, ds, b, s).start()
+                res_copy(db, ds, b, s).start()
     for quarter in range(4):
         own[6 + quarter].wait()
     for source in (near, inner, outer):

time: 77.2 us -> 81.9 us (1.061)
  the two profiles are of different devices: /device:TPU:0 before, /device:TPU:4 now
where the time goes in v5:
time: 81.9 us; the launch traced here: 81.7 us
  Pallas kernels  79.8 us (97%)
  local copies, waits for them, and re-layouts  1.87 us (2%)
    pallas_call x1, Pallas kernels, fused(): pl.pallas_call(fused_kernel, out_shape=jax.ShapeDtypeStruct((4, 512, 128)...  79.8 us
    unnamed x1, local copies, waits for them, and re-layouts  1.87 us

profile of v5, /device:TPU:4, one launch (start us, length us, event | category | flops | bytes accessed | tf_op | source)
XLA Modules:
  0.0 81.7 jit_solution(4790681415041048405)
XLA Ops:
  0.0 79.8 %shard_map.100 = bf16[4,512,128]{2,1,0:T(8,128)(2,1)} custom-call(bf16[3,4,4,2,2,32,128]{6,5,4,3,2,1,0:T(8,128)(2,1)} %bitcast.11, bf16[4,2,8,32,128]{4,3,2,1,0:T(8,128)(2,1)} %bitcast.12, bf16[4,128,2048]{2,1,0:T(8,128)(2,1)} %bitcast.9, f32[4,32,64]{2,1,0:T(8,128)} %bitcast.15, f32[3,4,2048]{2,1,0:T(4,128)} %mod_in.1, bf16[64,2048]{1,0:T(8,128)(2,1)} %bitcast.14, ...), custom_call_target="tpu_custom_call" | custom-call | tf_op jit(solution)/shard_map/pallas_call | solution.py:526
  79.8 1.9 %copy.12 = bf16[1,4,512,128]{3,2,1,0:T(8,128)(2,1)} copy(bf16[1,4,512,128]{3,2,1,0:T(8,128)(2,1)} %bitcast.10) | data formatting | bytes 1048576
